TPU v7x, 768 devices: a whole 4x8x12 slice. The times are simulated.
768 devices in a mesh: rep: 192 (over x_hi, z, y), fsdp: 4 (over x_lo, core).
Axes of the slice: x: 4 (x_hi: 2, x_lo: 2; x = x_hi * 2 + x_lo), y: 8, z: 12, core: 2. Of those that a mesh axis runs over, the one named last changes fastest.
Arguments:
- gradient: bfloat16 [192, 4, 128, 5120], P('rep', 'fsdp'), may hold values from -6 to 6
- momentum: float32 [192, 128, 5120], P('rep', None, 'fsdp'), may hold values from -6 to 6
- params: float32 [128, 5120], P(None, 'fsdp'), may hold values from -6 to 6
Outputs:
- new_params: float32 [128, 5120], P(None, 'fsdp')
- new_momentum: float32 [192, 128, 5120], P('rep', None, 'fsdp')
All inputs are finite; a program needn't handle non-finite values.
Results may differ from a plain program's by a relative error of at most 0.0003.
Values sent between devices are 32-bit elements; how exact they have to be, the bound alone decides.
A program may use at most 64 MiB of HBM per device.

v0:
```python
import jax
import jax.numpy as jnp
from jax import lax
from jax.sharding import PartitionSpec as P

TILE = 128
KEEP = 32


def make_basis(keep, tile):
    k = jnp.arange(keep, dtype=jnp.float32)[:, None]
    n = jnp.arange(tile, dtype=jnp.float32)[None, :]
    table = jnp.cos(jnp.pi * (2.0 * n + 1.0) * k / (2.0 * tile)) * jnp.sqrt(2.0 / tile)
    return table * jnp.where(k == 0, jnp.sqrt(0.5), 1.0)


def encode(matrix, basis, tile):
    tiles = matrix.reshape(matrix.shape[0] // tile, tile, matrix.shape[1] // tile, tile)
    return jnp.einsum("kr,arbc,lc->abkl", basis, tiles, basis, precision=lax.Precision.HIGHEST)


def decode(coefs, basis, tile):
    tiles = jnp.einsum("kr,abkl,lc->arbc", basis, coefs, basis, precision=lax.Precision.HIGHEST)
    return tiles.reshape(tiles.shape[0] * tile, tiles.shape[2] * tile)


def per_device(gradient, momentum, params):
    basis = make_basis(KEEP, TILE)
    reduced = lax.psum_scatter(
        gradient.astype(jnp.float32), "fsdp", scatter_dimension=3, tiled=True
    )[0, 0]
    moment = 0.9 * momentum[0] + reduced
    coefs = encode(moment, basis, TILE)
    new_moment = moment - decode(coefs, basis, TILE)
    tile_rows, tile_cols = (coefs.shape[0], coefs.shape[1])
    flat = coefs.reshape(1, tile_rows * tile_cols, KEEP * KEEP)
    total = lax.psum(flat, "rep")[0]
    total = total.reshape(tile_rows, tile_cols, KEEP, KEEP)
    scale = 1.0 / jnp.sqrt(jnp.float32(lax.axis_size("rep")))
    new_params = params - scale * decode(total, basis, TILE)
    return (new_params, new_moment[None])


def solution(mesh):
    in_specs = (P("rep", "fsdp", None, None), P("rep", None, "fsdp"), P(None, "fsdp"))
    out_specs = (P(None, "fsdp"), P("rep", None, "fsdp"))
    return jax.shard_map(
        per_device, mesh=mesh, in_specs=in_specs, out_specs=out_specs, check_vma=False
    )
```

profile of v0, /device:TPU:2, one launch (start us, length us, event | category | flops | bytes accessed | tf_op | source)
XLA Modules:
  0.0 1130.2 jit_solution(17739301812619895110)
XLA Ops:
  7.2 0.0 reduce-scatter.2.cloned.1.call-start
  7.2 1.8 copy.8
  9.0 1.7 convert_element_type.3
  10.7 0.0 copy-start.1
  10.7 0.0 reduce-scatter.2.cloned.1.call-update
  10.7 1.1 copy-done.1
  11.8 0.2 copy.7
  12.0 0.1 broadcast_multiply_fusion
  12.1 44.7 %reduce-scatter.2.cloned.1.call-done = f32[1,1,128,1280]{2,3,1,0:T(8,128)} async-done(((f32[1,1,128,5120]{2,3,1,0:T(8,128)}), f32[1,1,128,1280]{2,3,1,0:T(8,128)}) %reduce-scatter.2.cloned.1.call-update) | async-done | bytes 655376 | tf_op jit(solution)/shard_map/reduce_scatter | solution.py:29
  56.8 0.0 copy-start
  56.8 2.0 fusion
  58.8 0.4 fusion.9
  59.2 0.5 fusion.4
  59.6 1059.4 %psum.7 = f32[10,32,32]{2,1,0:T(8,128)S(1)} all-reduce(f32[10,32,32]{2,1,0:T(8,128)S(1)} %fusion.9), channel_id=1, replica_groups=mesh['rep'=192,'fsdp'=4] {'rep'}, use_global_device_ids=true, to_apply=%region_1.2 | all-reduce | flops 10240 | bytes 81920 | tf_op jit(solution)/shard_map/psum | solution.py:37
  1119.0 0.8 fusion.2
  1119.8 0.0 copy-done
  1119.8 0.1 bitcast_subtract_fusion
  1119.9 1.1 copy.10
  1121.0 0.0 copy-start.2
  1121.0 0.5 fusion.7
  1121.4 0.8 convolution_multiply_fusion
  1122.2 0.2 copy.9
  1122.5 0.0 copy-done.2
  1122.5 0.9 sub.7
  (2 shorter events, 0.0 us)
Async XLA Ops:
  7.2 49.6 %reduce-scatter.2.cloned.1.call-start = ((), (), s32[]{:S(2)}) async-start(), calls=%async_computation.1 | async-start | bytes 3276800 | tf_op jit(solution)/shard_map/reduce_scatter | solution.py:29
  10.7 1.1 copy-start.1
  56.8 1063.0 %copy-start = (f32[1,1,128,1280]{2,3,1,0:T(8,128)S(1)}, f32[1,1,128,1280]{2,3,1,0:T(8,128)}, u32[]{:S(2)}) copy-start(f32[1,1,128,1280]{2,3,1,0:T(8,128)} %reduce-scatter.2.cloned.1.call-done) | copy-start | bytes 1966084
  1121.0 1.5 copy-start.2
Sparse Core Ops, SparseCore 0:
  11.1 45.6 reduce-scatter.1
where the time goes:
time: 1130 us
  blocking collectives  1060 us (94%)
  waiting for transfers between devices  44.7 us (4%)
  between operations  14.1 us (1%)
    psum x1, blocking collectives, per_device(): total = lax.psum(flat, 'rep')[0]  1060 us
    reduce_scatter x1, waiting for transfers between devices, per_device(): lax.psum_scatter(gradient.astype(jnp.float32), 'fsdp', scatter_dimension=...  44.7 us
  transfers between devices with their start and end apart: 1, of which 1 were waited for; matrix products, arithmetic and copies ran while one was open for 0% of the time, Pallas kernels for 0%

commit v1 on v0

v1 whole, which is shorter than its diff:
```python
import jax
import jax.numpy as jnp
import numpy as np
from jax import lax
from jax.experimental import pallas as pl
from jax.experimental.pallas import tpu as pltpu
from jax.sharding import PartitionSpec as P

MESH = pl.DeviceIdType.MESH
F32, BF16 = jnp.float32, jnp.bfloat16
TILE, KEEP = 128, 32
NXH, NZ, NY = 2, 12, 8
ROWS_XY = [(0, 3), (0, 4), (0, 5), (0, 6), (1, 2), (1, 3), (1, 4), (1, 5), (1, 6), (1, 7)]
NT = 10


def split_np(a):
    a = np.asarray(a, np.float32)
    high = a.astype(jnp.bfloat16)
    low = (a - high.astype(np.float32)).astype(jnp.bfloat16)
    return high, low


def constants():
    k, n = np.arange(KEEP)[:, None], np.arange(TILE)[None, :]
    basis = np.cos(np.pi * (2 * n + 1) * k / (2 * TILE)) * np.sqrt(2 / TILE)
    basis = basis * np.where(k == 0, np.sqrt(0.5), 1.0)
    b1, b2 = split_np(basis)
    zero = np.zeros_like(b1)

    def four(b):
        out = np.zeros((4 * b.shape[0], 4 * b.shape[1]), b.dtype)
        for i in range(4):
            out[i * b.shape[0] : (i + 1) * b.shape[0], i * b.shape[1] : (i + 1) * b.shape[1]] = b
        return out

    right = np.concatenate([four(b1.T), four(b2.T)], 1)
    left = np.block([[b1, b1], [b2, zero]])
    p1, p2 = split_np(basis.T @ basis)
    p_left = np.concatenate([p1, p1, p2], 1)
    p_right = np.concatenate([p1, p1, p2], 0)
    d_left = np.concatenate([b1.T, b1.T, b2.T], 1)
    d_right = np.concatenate([four(b1), four(b1), four(b2)], 0)
    return right, left, p_left, p_right, d_left, d_right


def split(x):
    high = x.astype(BF16)
    return high, (x - high.astype(F32)).astype(BF16)


def dot(a, b):
    return jnp.dot(a, b, preferred_element_type=F32)


def columns_of(g, right, low):
    parts = []
    for q in range(3):
        width = 512 if q < 2 else 256
        x = g[:, 512 * q : 512 * q + width]
        if low:
            y = dot(x, right[:width, :])
            parts.append(y[:, :128] + y[:, 128:])
        else:
            parts.append(dot(x, right[:width, :128]))
    return jnp.concatenate(parts, 1)


def rows_of(y, left):
    y1, y2 = split(y)
    z = dot(left, jnp.concatenate([y1, y2], 0))
    return z[:KEEP] + z[KEEP:]


def chunks_of(z):
    tail = z[:, 256:384]
    tail = tail[:16] + pltpu.roll(tail[16:], 64, 1)
    return (
        z[:, :128].reshape(4, 8, 128),
        z[:, 128:256].reshape(4, 8, 128),
        tail.reshape(2, 8, 128),
    )


def kernel(
    scale, g_hbm, m_hbm, w_hbm, c_right, c_left, c_pl, c_pr, c_dl, c_dr,
    new_w, new_m,
    gs, ms, ws, right, left, p_left, p_right, d_left, d_right,
    cf, rc, sa, ra, sb, rb, sc, rt,
    gst, rg, xs, xt, om, ow,
    load_sem, core_s, core_r, a_sem, b_sem, c_sem, x_s, x_r, out_sem,
):
    rep, f = lax.axis_index("rep"), lax.axis_index("fsdp")
    xh, z, y = rep // (NZ * NY), (rep // NY) % NZ, rep % NY
    xl, c = f // 2, f % 2

    def device(dxh, dz, dy, dxl, dc):
        return ((dxh * NZ + dz) * NY + dy, dxl * 2 + dc)

    sibling = device(xh, z, y, xl, 1 - c)
    across = device(xh, z, y, 1 - xl, c)
    owner = jnp.logical_or(
        jnp.logical_and(xh == 0, jnp.logical_and(y >= 3, y <= 6)),
        jnp.logical_and(xh == 1, y >= 2),
    )
    mine = jnp.where(owner, jnp.where(xh == 0, y - 3, y + 2), 0)
    chip = (xh * NY + y) * 2 + xl

    blocks = [f, (1 - xl) * 2 + c, xl * 2 + 1 - c, (1 - xl) * 2 + 1 - c]
    loads = [
        pltpu.make_async_copy(
            g_hbm.at[0, 0, :, pl.ds(pl.multiple_of(b * 1280, 1280), 1280)], gs.at[i], load_sem.at[i]
        )
        for i, b in enumerate(blocks)
    ]
    consts = [
        pltpu.make_async_copy(src, dst, load_sem.at[4 + i])
        for i, (src, dst) in enumerate(
            [(c_right, right), (c_left, left), (m_hbm.at[0], ms), (c_pl, p_left), (c_pr, p_right),
             (c_dl, d_left), (c_dr, d_right), (w_hbm, ws)]
        )
    ]
    for copy in consts[:1] + loads + consts[1:]:
        copy.start()

    barrier = pltpu.get_barrier_semaphore()

    def greet(to):
        pl.semaphore_signal(barrier, inc=1, device_id=to, device_id_type=MESH)

    greet(sibling)
    for dx in range(2):
        for dy in range(NY):
            for dl in range(2):
                if dx or dy or dl:
                    greet(device((xh + dx) % 2, z, (y + dy) % NY, (xl + dl) % 2, c))

    @pl.when(owner)
    def _():
        for dz in range(1, NZ):
            greet(device(xh, (z + dz) % NZ, y, xl, c))

    consts[0].wait()
    ys = []
    for i in (2, 3):
        loads[i].wait()
        ys.append(columns_of(gs[i], right, True))
    consts[1].wait()
    zs = rows_of(jnp.concatenate(ys, 1), left[...])
    for i in (2, 3):
        q = chunks_of(zs[:, 384 * (i - 2) : 384 * (i - 1)])
        cf[i, 0:4], cf[i, 4:8], cf[i, 8:10] = q

    @pl.when(owner)
    def _():
        pl.semaphore_wait(barrier, 32 + NZ - 1)

    @pl.when(jnp.logical_not(owner))
    def _():
        pl.semaphore_wait(barrier, 32)

    def send(src, dst, s, r, to):
        return pltpu.make_async_remote_copy(
            src_ref=src, dst_ref=dst, send_sem=s, recv_sem=r, device_id=to, device_id_type=MESH
        )

    core0 = send(cf.at[pl.ds(2, 2)], rc, core_s.at[0], core_r.at[0], sibling)
    core0.start()
    for t in range(NT):
        gst[0, t] = gs[3, :, 128 * t : 128 * t + 128].astype(F32)
    core1 = send(gst.at[0], rg.at[0], core_s.at[1], core_r.at[1], sibling)
    core1.start()
    ys = []
    for i in (0, 1):
        loads[i].wait()
        ys.append(columns_of(gs[i], right, True))
    consts[2].wait()
    m1, m2 = split(0.9 * ms[...])
    ys[0] = ys[0] + columns_of(m1, right, True) + columns_of(m2, right, False)
    zs = rows_of(jnp.concatenate(ys, 1), left[...])
    core0.wait_recv()
    for i in (0, 1):
        q = chunks_of(zs[:, 384 * i : 384 * (i + 1)])
        sa[i, 0:4] = q[0] + rc[i, 0:4]
        sa[i, 4:8] = q[1] + rc[i, 4:8]
        sa[i, 8:10] = q[2] + rc[i, 8:10]

    for i in range(2):
        for j, (ox, oy) in enumerate(ROWS_XY):
            to = device(ox, z, oy, xl if i == 0 else 1 - xl, c)
            copy = send(sa.at[i, j], ra.at[chip], a_sem.at[i], a_sem.at[2], to)
            if i == 0:
                here = jnp.logical_and(xh == ox, y == oy)

                @pl.when(jnp.logical_not(here))
                def _():
                    copy.start()

                @pl.when(here)
                def _():
                    ra[chip] = sa[0, j]
            else:
                copy.start()

    for t in range(NT):
        gst[1, t] = gs[2, :, 128 * t : 128 * t + 128].astype(F32)
    core2 = send(gst.at[1], rg.at[1], core_s.at[2], core_r.at[2], sibling)
    core2.start()
    core1.wait_recv()
    swaps = []
    for t in range(NT):
        xs[t] = gs[1, :, 128 * t : 128 * t + 128].astype(F32) + rg[0, t]
        swaps.append(send(xs.at[t], xt.at[t], x_s.at[t], x_r.at[t], across))
        swaps[-1].start()

    @pl.when(owner)
    def _():
        send(ra.at[pl.ds(0, 31)], ra.at[pl.ds(0, 31)], a_sem.at[0], a_sem.at[2], sibling).wait_recv()
        total = ra[0]
        for i in range(1, 32):
            total = total + ra[i]
        sb[...] = total
        rb[z] = total
        for dz in list(range(1, 7)) + list(range(11, 6, -1)):
            send(sb, rb.at[z], b_sem.at[0], b_sem.at[1], device(xh, (z + dz) % NZ, y, xl, c)).start()
        send(rb.at[pl.ds(0, 11)], rb.at[pl.ds(0, 11)], b_sem.at[0], b_sem.at[1], sibling).wait_recv()
        total = rb[0]
        for i in range(1, NZ):
            total = total + rb[i]
        sc[...] = total
        rt[mine] = total
        for dx in range(2):
            for dy in range(NY):
                if dx or dy:
                    to = device((xh + dx) % 2, z, (y + dy) % NY, xl, c)
                    send(sc, rt.at[mine], c_sem.at[0], c_sem.at[1], to).start()

    core2.wait_recv()
    consts[3].wait()
    consts[4].wait()
    outs = []
    for t in range(NT):
        cols = pl.ds(128 * t, 128)
        swaps[t].wait_recv()
        x = 0.9 * ms[:, cols] + ((gs[0, :, cols].astype(F32) + rg[1, t]) + xt[t])
        x1, x2 = split(x)
        u1, u2 = split(dot(p_left[...], jnp.concatenate([x1, x2, x1], 0)))
        om[:, cols] = x - dot(jnp.concatenate([u1, u2, u1], 1), p_right[...])
        outs.append(pltpu.make_async_copy(om.at[:, cols], new_m.at[0, :, cols], out_sem.at[t]))
        outs[-1].start()

    for i in range(5, 8):
        consts[i].wait()

    @pl.when(owner)
    def _():
        send(rt.at[pl.ds(0, 9)], rt.at[pl.ds(0, 9)], c_sem.at[0], c_sem.at[1], sibling).wait_recv()

    @pl.when(jnp.logical_not(owner))
    def _():
        send(rt, rt, c_sem.at[0], c_sem.at[1], sibling).wait_recv()

    tail = rt[8:10].reshape(16, 128)
    zt = jnp.concatenate(
        [rt[0:4].reshape(32, 128), rt[4:8].reshape(32, 128), jnp.concatenate([tail, pltpu.roll(tail, 64, 1)], 0)], 1
    )
    z1, z2 = split(zt)
    v1, v2 = split(dot(d_left[...], jnp.concatenate([z1, z2, z1], 0)))
    for q in range(3):
        width = 512 if q < 2 else 256
        part = slice(128 * q, 128 * q + 128)
        low = dot(jnp.concatenate([v1[:, part], v2[:, part], v1[:, part]], 1), d_right[:, :width])
        cols = pl.ds(512 * q, width)
        ow[:, cols] = ws[:, cols] - scale * low
        outs.append(pltpu.make_async_copy(ow.at[:, cols], new_w.at[:, cols], out_sem.at[NT + q]))
        outs[-1].start()

    for copy in (core0, core1, core2, *swaps):
        copy.wait_send()
    send(sa.at[1], sa.at[1], a_sem.at[1], a_sem.at[2], sibling).wait_send()

    @pl.when(owner)
    def _():
        send(sa.at[0, pl.ds(0, 9)], sa.at[0, pl.ds(0, 9)], a_sem.at[0], a_sem.at[2], sibling).wait_send()
        send(rb.at[pl.ds(0, 11)], rb.at[pl.ds(0, 11)], b_sem.at[0], b_sem.at[1], sibling).wait_send()
        send(ra.at[pl.ds(0, 15)], ra.at[pl.ds(0, 15)], c_sem.at[0], c_sem.at[1], sibling).wait_send()

    @pl.when(jnp.logical_not(owner))
    def _():
        send(sa.at[0], sa.at[0], a_sem.at[0], a_sem.at[2], sibling).wait_send()

    for copy in outs:
        copy.wait()


def solution(mesh):
    scale = float(1.0 / np.sqrt(np.float32(mesh.shape["rep"])))
    consts = constants()

    def per_device(gradient, momentum, params):
        vmem, dma = pltpu.VMEM, pltpu.SemaphoreType.DMA
        tiles = (NT, TILE, TILE)
        chunk = (8, 128)
        slab = (TILE, NT * TILE)

        def body(*refs):
            kernel(scale, *refs)

        new_w, new_m = pl.pallas_call(
            body,
            out_shape=(
                jax.ShapeDtypeStruct(params.shape, F32),
                jax.ShapeDtypeStruct(momentum.shape, F32),
            ),
            in_specs=[pl.BlockSpec(memory_space=pl.ANY)] * 9,
            out_specs=(pl.BlockSpec(memory_space=pl.ANY),) * 2,
            scratch_shapes=[
                vmem((4, *slab), BF16), vmem(slab, F32), vmem(slab, F32),
                *[vmem(a.shape, BF16) for a in consts],
                vmem((4, NT, *chunk), F32),
                vmem((2, NT, *chunk), F32),
                vmem((2, NT, *chunk), F32),
                vmem((32, *chunk), F32),
                vmem(chunk, F32),
                vmem((NZ, *chunk), F32),
                vmem(chunk, F32),
                vmem((NT, *chunk), F32),
                vmem((2, *tiles), F32),
                vmem((2, *tiles), F32),
                vmem(tiles, F32),
                vmem(tiles, F32),
                vmem(slab, F32),
                vmem(slab, F32),
                dma((12,)), dma((3,)), dma((3,)), dma((3,)), dma((2,)), dma((2,)),
                dma((NT,)), dma((NT,)), dma((NT + 3,)),
            ],
            compiler_params=pltpu.CompilerParams(
                collective_id=0, has_side_effects=True, vmem_limit_bytes=40 * 2**20
            ),
        )(gradient, momentum, params, *[jnp.asarray(a) for a in consts])
        return new_w, new_m

    return jax.shard_map(
        per_device,
        mesh=mesh,
        in_specs=(P("rep", "fsdp", None, None), P("rep", None, "fsdp"), P(None, "fsdp")),
        out_specs=(P(None, "fsdp"), P("rep", None, "fsdp")),
        check_vma=False,
    )
```

time: 1130 us -> 52.5 us (0.05)
  the two profiles are of different devices: /device:TPU:2 before, /device:TPU:8 now
where the time goes in v1:
time: 52.5 us; the launch traced here: 51.9 us
  Pallas kernels  40.9 us (78%)
  local copies, waits for them, and re-layouts  10.4 us (20%)
  between operations  0.66 us (1%)
    pallas_call x1, Pallas kernels, per_device(): pl.pallas_call(body, out_shape=(jax.ShapeDtypeStruct(params.shape, F32),...  40.9 us
    unnamed x20, local copies, waits for them, and re-layouts  10.4 us

profile of v1, /device:TPU:8, one launch (start us, length us, event | category | flops | bytes accessed | tf_op | source)
XLA Modules:
  0.0 51.9 jit_solution(7871836924833593535)
XLA Ops:
  0.6 0.0 copy-start
  0.6 1.3 %copy-done = bf16[1,1,128,5120]{3,2,1,0:T(8,128)(2,1)S(1)} copy-done((bf16[1,1,128,5120]{3,2,1,0:T(8,128)(2,1)S(1)}, bf16[1,1,128,5120]{3,2,1,0:T(8,128)(2,1)}, u32[]{:S(2)}) %copy-start) | copy-done | bytes 1310744
  1.9 0.0 copy-start.1
  1.9 1.1 %copy-done.1 = f32[1,128,1280]{2,1,0:T(8,128)S(1)} copy-done((f32[1,128,1280]{2,1,0:T(8,128)S(1)}, f32[1,128,1280]{2,1,0:T(8,128)}, u32[]{:S(2)}) %copy-start.1) | copy-done | bytes 655384
  3.0 0.0 copy-start.2
  3.0 1.1 %copy-done.2 = f32[128,1280]{1,0:T(8,128)S(1)} copy-done((f32[128,1280]{1,0:T(8,128)S(1)}, f32[128,1280]{1,0:T(8,128)}, u32[]{:S(2)}) %copy-start.2) | copy-done | bytes 655384
  4.1 0.0 copy-start.3
  4.1 1.0 %copy-done.3 = bf16[384,512]{1,0:T(8,128)(2,1)S(1)} copy-done((bf16[384,512]{1,0:T(8,128)(2,1)S(1)}, bf16[384,512]{1,0:T(8,128)(2,1)}, u32[]{:S(2)}) %copy-start.3) | copy-done | bytes 393240
  5.1 0.0 copy-start.4
  5.1 0.9 %copy-done.4 = bf16[512,256]{1,0:T(8,128)(2,1)S(1)} copy-done((bf16[512,256]{1,0:T(8,128)(2,1)S(1)}, bf16[512,256]{1,0:T(8,128)(2,1)}, u32[]{:S(2)}) %copy-start.4) | copy-done | bytes 262168
  6.1 0.0 copy-start.5
  6.1 0.9 %copy-done.5 = bf16[384,128]{1,0:T(8,128)(2,1)S(1)} copy-done((bf16[384,128]{1,0:T(8,128)(2,1)S(1)}, bf16[384,128]{1,0:T(8,128)(2,1)}, u32[]{:S(2)}) %copy-start.5) | copy-done | bytes 98328
  7.0 0.0 copy-start.6
  7.0 0.9 %copy-done.6 = bf16[128,384]{1,0:T(8,128)(2,1)S(1)} copy-done((bf16[128,384]{1,0:T(8,128)(2,1)S(1)}, bf16[128,384]{1,0:T(8,128)(2,1)}, u32[]{:S(2)}) %copy-start.6) | copy-done | bytes 98328
  7.9 0.0 copy-start.7
  7.9 0.8 %copy-done.7 = bf16[128,96]{1,0:T(8,128)(2,1)S(1)} copy-done((bf16[128,96]{1,0:T(8,128)(2,1)S(1)}, bf16[128,96]{1,0:T(8,128)(2,1)}, u32[]{:S(2)}) %copy-start.7) | copy-done | bytes 24600
  8.6 0.0 copy-start.8
  8.6 0.8 %copy-done.8 = bf16[64,256]{1,0:T(8,128)(2,1)S(1)} copy-done((bf16[64,256]{1,0:T(8,128)(2,1)S(1)}, bf16[64,256]{1,0:T(8,128)(2,1)}, u32[]{:S(2)}) %copy-start.8) | copy-done | bytes 32792
  9.4 40.9 %shard_map.104 = (f32[128,1280]{1,0:T(8,128)S(1)}, f32[1,128,1280]{2,1,0:T(8,128)S(1)}) custom-call(bf16[1,1,128,5120]{3,2,1,0:T(8,128)(2,1)S(1)} %copy-done, f32[1,128,1280]{2,1,0:T(8,128)S(1)} %copy-done.1, f32[128,1280]{1,0:T(8,128)S(1)} %copy-done.2, bf16[512,256]{1,0:T(8,128)(2,1)S(1)} %copy-done.4, bf16[64,256]{1,0:T(8,128)(2,1)S(1)} %copy-done.8, ...), custom_call_target="tpu_custom_call" | custom-call | tf_op jit(solution)/shard_map/pallas_call | solution.py:309
  50.3 0.8 %copy.13 = f32[128,1280]{1,0:T(8,128)} copy(f32[128,1280]{1,0:T(8,128)S(1)} %get-tuple-element.4) | data formatting | bytes 1310720
  51.1 0.8 %copy.14 = f32[1,128,1280]{2,1,0:T(8,128)} copy(f32[1,128,1280]{2,1,0:T(8,128)S(1)} %get-tuple-element.5) | data formatting | bytes 1310720
Async XLA Ops:
  0.6 1.3 %copy-start = (bf16[1,1,128,5120]{3,2,1,0:T(8,128)(2,1)S(1)}, bf16[1,1,128,5120]{3,2,1,0:T(8,128)(2,1)}, u32[]{:S(2)}) copy-start(bf16[1,1,128,5120]{3,2,1,0:T(8,128)(2,1)} %refs_0_.1) | copy-start | bytes 3932164
  1.9 1.1 %copy-start.1 = (f32[1,128,1280]{2,1,0:T(8,128)S(1)}, f32[1,128,1280]{2,1,0:T(8,128)}, u32[]{:S(2)}) copy-start(f32[1,128,1280]{2,1,0:T(8,128)} %refs_1_.1) | copy-start | bytes 1966084
  3.0 1.1 %copy-start.2 = (f32[128,1280]{1,0:T(8,128)S(1)}, f32[128,1280]{1,0:T(8,128)}, u32[]{:S(2)}) copy-start(f32[128,1280]{1,0:T(8,128)} %refs_2_.1) | copy-start | bytes 1966084
  4.1 1.0 %copy-start.3 = (bf16[384,512]{1,0:T(8,128)(2,1)S(1)}, bf16[384,512]{1,0:T(8,128)(2,1)}, u32[]{:S(2)}) copy-start(bf16[384,512]{1,0:T(8,128)(2,1)} %constant.17.clone.refs_8_) | copy-start | bytes 1179652
  5.1 0.9 %copy-start.4 = (bf16[512,256]{1,0:T(8,128)(2,1)S(1)}, bf16[512,256]{1,0:T(8,128)(2,1)}, u32[]{:S(2)}) copy-start(bf16[512,256]{1,0:T(8,128)(2,1)} %constant.12.clone.refs_3_) | copy-start | bytes 786436
  6.1 0.9 %copy-start.5 = (bf16[384,128]{1,0:T(8,128)(2,1)S(1)}, bf16[384,128]{1,0:T(8,128)(2,1)}, u32[]{:S(2)}) copy-start(bf16[384,128]{1,0:T(8,128)(2,1)} %constant.15.clone.refs_6_) | copy-start | bytes 294916
  7.0 0.9 %copy-start.6 = (bf16[128,384]{1,0:T(8,128)(2,1)S(1)}, bf16[128,384]{1,0:T(8,128)(2,1)}, u32[]{:S(2)}) copy-start(bf16[128,384]{1,0:T(8,128)(2,1)} %constant.14.clone.refs_5_) | copy-start | bytes 294916
  7.9 0.8 %copy-start.7 = (bf16[128,96]{1,0:T(8,128)(2,1)S(1)}, bf16[128,96]{1,0:T(8,128)(2,1)}, u32[]{:S(2)}) copy-start(bf16[128,96]{1,0:T(8,128)(2,1)} %constant.16.clone.refs_7_) | copy-start | bytes 73732
  8.6 0.8 %copy-start.8 = (bf16[64,256]{1,0:T(8,128)(2,1)S(1)}, bf16[64,256]{1,0:T(8,128)(2,1)}, u32[]{:S(2)}) copy-start(bf16[64,256]{1,0:T(8,128)(2,1)} %constant.13.clone.refs_4_) | copy-start | bytes 98308

commit v2 on v1

--- a/solution.py
+++ b/solution.py
@@ -10,7 +10,8 @@
 F32, BF16 = jnp.float32, jnp.bfloat16
 TILE, KEEP = 128, 32
 NXH, NZ, NY = 2, 12, 8
-ROWS_XY = [(0, 3), (0, 4), (0, 5), (0, 6), (1, 2), (1, 3), (1, 4), (1, 5), (1, 6), (1, 7)]
+FIRST, LINES = 7, 5
+ROWS_XY = [(i, (FIRST + j) % NY) for i in range(NXH) for j in range(LINES)]
 NT = 10
 
 
@@ -83,12 +84,12 @@
 
 
 def kernel(
-    scale, g_hbm, m_hbm, w_hbm, c_right, c_left, c_pl, c_pr, c_dl, c_dr,
-    new_w, new_m,
-    gs, ms, ws, right, left, p_left, p_right, d_left, d_right,
+    g_hbm, m_hbm, c_right, c_left, c_pl, c_pr,
+    totals, new_m,
+    gs, ms, right, left, p_left, p_right,
     cf, rc, sa, ra, sb, rb, sc, rt,
-    gst, rg, xs, xt, om, ow,
-    load_sem, core_s, core_r, a_sem, b_sem, c_sem, x_s, x_r, out_sem,
+    gst, rg, xs, xt, om,
+    load_sem, core_s, core_r, a_sem, b_sem, c_sem, x_s, x_r, out_sem, in_sem,
 ):
     rep, f = lax.axis_index("rep"), lax.axis_index("fsdp")
     xh, z, y = rep // (NZ * NY), (rep // NY) % NZ, rep % NY
@@ -99,11 +100,9 @@
 
     sibling = device(xh, z, y, xl, 1 - c)
     across = device(xh, z, y, 1 - xl, c)
-    owner = jnp.logical_or(
-        jnp.logical_and(xh == 0, jnp.logical_and(y >= 3, y <= 6)),
-        jnp.logical_and(xh == 1, y >= 2),
-    )
-    mine = jnp.where(owner, jnp.where(xh == 0, y - 3, y + 2), 0)
+    line = (y - FIRST + NY) % NY
+    owner = line < LINES
+    mine = jnp.where(owner, xh * LINES + line, 0)
     chip = (xh * NY + y) * 2 + xl
 
     blocks = [f, (1 - xl) * 2 + c, xl * 2 + 1 - c, (1 - xl) * 2 + 1 - c]
@@ -116,8 +115,7 @@
     consts = [
         pltpu.make_async_copy(src, dst, load_sem.at[4 + i])
         for i, (src, dst) in enumerate(
-            [(c_right, right), (c_left, left), (m_hbm.at[0], ms), (c_pl, p_left), (c_pr, p_right),
-             (c_dl, d_left), (c_dr, d_right), (w_hbm, ws)]
+            [(c_right, right), (c_left, left), (m_hbm.at[0], ms), (c_pl, p_left), (c_pr, p_right)]
         )
     ]
     for copy in consts[:1] + loads + consts[1:]:
@@ -125,20 +123,26 @@
 
     barrier = pltpu.get_barrier_semaphore()
 
-    def greet(to):
-        pl.semaphore_signal(barrier, inc=1, device_id=to, device_id_type=MESH)
-
-    greet(sibling)
-    for dx in range(2):
-        for dy in range(NY):
-            for dl in range(2):
-                if dx or dy or dl:
-                    greet(device((xh + dx) % 2, z, (y + dy) % NY, (xl + dl) % 2, c))
+    def signal(to, sem):
+        pl.semaphore_signal(sem, inc=1, device_id=to, device_id_type=MESH)
 
     @pl.when(owner)
     def _():
-        for dz in range(1, NZ):
-            greet(device(xh, (z + dz) % NZ, y, xl, c))
+        for dy in (4, 3, 5, 2, 6, 1, 7, 0):
+            for dx in range(2):
+                for dl in range(2):
+                    if dx or dy or dl:
+                        signal(device((xh + dx) % 2, z, (y + dy) % NY, (xl + dl) % 2, 0), barrier)
+        for dz in (6, 5, 7, 4, 8, 3, 9, 2, 10, 1, 11):
+            signal(device(xh, (z + dz) % NZ, y, xl, 1), barrier)
+
+    @pl.when(jnp.logical_not(owner))
+    def _():
+        signal(device(xh, z, y, 1 - xl, 0), barrier)
+
+    @pl.when(c == 1)
+    def _():
+        signal(sibling, barrier)
 
     consts[0].wait()
     ys = []
@@ -151,13 +155,21 @@
         q = chunks_of(zs[:, 384 * (i - 2) : 384 * (i - 1)])
         cf[i, 0:4], cf[i, 4:8], cf[i, 8:10] = q
 
-    @pl.when(owner)
-    def _():
-        pl.semaphore_wait(barrier, 32 + NZ - 1)
-
-    @pl.when(jnp.logical_not(owner))
-    def _():
-        pl.semaphore_wait(barrier, 32)
+    @pl.when(c == 0)
+    def _():
+        @pl.when(owner)
+        def _():
+            pl.semaphore_wait(barrier, 4 * NT - 1)
+
+        @pl.when(jnp.logical_not(owner))
+        def _():
+            pl.semaphore_wait(barrier, 4 * NT + 3)
+
+        signal(sibling, in_sem.at[0])
+
+    @pl.when(c == 1)
+    def _():
+        pl.semaphore_wait(in_sem.at[0], 1)
 
     def send(src, dst, s, r, to):
         return pltpu.make_async_remote_copy(
@@ -213,6 +225,11 @@
         swaps.append(send(xs.at[t], xt.at[t], x_s.at[t], x_r.at[t], across))
         swaps[-1].start()
 
+    @pl.when(jnp.logical_and(owner, c == 1))
+    def _():
+        pl.semaphore_wait(barrier, 2 * (NZ - 1))
+        signal(sibling, in_sem.at[1])
+
     @pl.when(owner)
     def _():
         send(ra.at[pl.ds(0, 31)], ra.at[pl.ds(0, 31)], a_sem.at[0], a_sem.at[2], sibling).wait_recv()
@@ -221,6 +238,11 @@
             total = total + ra[i]
         sb[...] = total
         rb[z] = total
+
+        @pl.when(c == 0)
+        def _():
+            pl.semaphore_wait(in_sem.at[1], 1)
+
         for dz in list(range(1, 7)) + list(range(11, 6, -1)):
             send(sb, rb.at[z], b_sem.at[0], b_sem.at[1], device(xh, (z + dz) % NZ, y, xl, c)).start()
         send(rb.at[pl.ds(0, 11)], rb.at[pl.ds(0, 11)], b_sem.at[0], b_sem.at[1], sibling).wait_recv()
@@ -249,9 +271,6 @@
         outs.append(pltpu.make_async_copy(om.at[:, cols], new_m.at[0, :, cols], out_sem.at[t]))
         outs[-1].start()
 
-    for i in range(5, 8):
-        consts[i].wait()
-
     @pl.when(owner)
     def _():
         send(rt.at[pl.ds(0, 9)], rt.at[pl.ds(0, 9)], c_sem.at[0], c_sem.at[1], sibling).wait_recv()
@@ -260,35 +279,55 @@
     def _():
         send(rt, rt, c_sem.at[0], c_sem.at[1], sibling).wait_recv()
 
+    outs.append(pltpu.make_async_copy(rt, totals, out_sem.at[NT]))
+    outs[-1].start()
+
+    for copy in (core0, core1, core2, *swaps):
+        copy.wait_send()
+    send(sa.at[1], sa.at[1], a_sem.at[1], a_sem.at[2], sibling).wait_send()
+
+    @pl.when(owner)
+    def _():
+        send(sa.at[0, pl.ds(0, 9)], sa.at[0, pl.ds(0, 9)], a_sem.at[0], a_sem.at[2], sibling).wait_send()
+        send(rb.at[pl.ds(0, 11)], rb.at[pl.ds(0, 11)], b_sem.at[0], b_sem.at[1], sibling).wait_send()
+        send(ra.at[pl.ds(0, 15)], ra.at[pl.ds(0, 15)], c_sem.at[0], c_sem.at[1], sibling).wait_send()
+
+    @pl.when(jnp.logical_not(owner))
+    def _():
+        send(sa.at[0], sa.at[0], a_sem.at[0], a_sem.at[2], sibling).wait_send()
+
+    for copy in outs:
+        copy.wait()
+
+
+def finish(scale, totals, m_hbm, w_hbm, c_dl, c_dr, new_w, new_m, rt, vm, ws, d_left, d_right, ow, in_sem, out_sem):
+    cuts = [pl.ds(0, 512), pl.ds(512, 512), pl.ds(1024, 256)]
+    loads = [
+        pltpu.make_async_copy(src, dst, in_sem.at[i])
+        for i, (src, dst) in enumerate(
+            [(totals, rt), (c_dl, d_left), (c_dr, d_right), (w_hbm, ws), *[(m_hbm.at[0, :, n], vm.at[:, n]) for n in cuts]]
+        )
+    ]
+    for copy in loads:
+        copy.start()
+    for copy in loads[:4]:
+        copy.wait()
     tail = rt[8:10].reshape(16, 128)
     zt = jnp.concatenate(
         [rt[0:4].reshape(32, 128), rt[4:8].reshape(32, 128), jnp.concatenate([tail, pltpu.roll(tail, 64, 1)], 0)], 1
     )
     z1, z2 = split(zt)
     v1, v2 = split(dot(d_left[...], jnp.concatenate([z1, z2, z1], 0)))
-    for q in range(3):
-        width = 512 if q < 2 else 256
+    outs = []
+    for q, cols in enumerate(cuts):
+        loads[4 + q].wait()
+        outs.append(pltpu.make_async_copy(vm.at[:, cols], new_m.at[0, :, cols], out_sem.at[3 + q]))
+        outs[-1].start()
         part = slice(128 * q, 128 * q + 128)
-        low = dot(jnp.concatenate([v1[:, part], v2[:, part], v1[:, part]], 1), d_right[:, :width])
-        cols = pl.ds(512 * q, width)
+        low = dot(jnp.concatenate([v1[:, part], v2[:, part], v1[:, part]], 1), d_right[:, : cols.size])
         ow[:, cols] = ws[:, cols] - scale * low
-        outs.append(pltpu.make_async_copy(ow.at[:, cols], new_w.at[:, cols], out_sem.at[NT + q]))
+        outs.append(pltpu.make_async_copy(ow.at[:, cols], new_w.at[:, cols], out_sem.at[q]))
         outs[-1].start()
-
-    for copy in (core0, core1, core2, *swaps):
-        copy.wait_send()
-    send(sa.at[1], sa.at[1], a_sem.at[1], a_sem.at[2], sibling).wait_send()
-
-    @pl.when(owner)
-    def _():
-        send(sa.at[0, pl.ds(0, 9)], sa.at[0, pl.ds(0, 9)], a_sem.at[0], a_sem.at[2], sibling).wait_send()
-        send(rb.at[pl.ds(0, 11)], rb.at[pl.ds(0, 11)], b_sem.at[0], b_sem.at[1], sibling).wait_send()
-        send(ra.at[pl.ds(0, 15)], ra.at[pl.ds(0, 15)], c_sem.at[0], c_sem.at[1], sibling).wait_send()
-
-    @pl.when(jnp.logical_not(owner))
-    def _():
-        send(sa.at[0], sa.at[0], a_sem.at[0], a_sem.at[2], sibling).wait_send()
-
     for copy in outs:
         copy.wait()
 
@@ -303,20 +342,20 @@
         chunk = (8, 128)
         slab = (TILE, NT * TILE)
 
-        def body(*refs):
-            kernel(scale, *refs)
-
-        new_w, new_m = pl.pallas_call(
-            body,
+        def last(*refs):
+            finish(scale, *refs)
+
+        totals, new_m = pl.pallas_call(
+            kernel,
             out_shape=(
-                jax.ShapeDtypeStruct(params.shape, F32),
+                jax.ShapeDtypeStruct((NT, *chunk), F32),
                 jax.ShapeDtypeStruct(momentum.shape, F32),
             ),
-            in_specs=[pl.BlockSpec(memory_space=pl.ANY)] * 9,
+            in_specs=[pl.BlockSpec(memory_space=pl.ANY)] * 6,
             out_specs=(pl.BlockSpec(memory_space=pl.ANY),) * 2,
             scratch_shapes=[
-                vmem((4, *slab), BF16), vmem(slab, F32), vmem(slab, F32),
-                *[vmem(a.shape, BF16) for a in consts],
+                vmem((4, *slab), BF16), vmem(slab, F32),
+                *[vmem(a.shape, BF16) for a in consts[:4]],
                 vmem((4, NT, *chunk), F32),
                 vmem((2, NT, *chunk), F32),
                 vmem((2, NT, *chunk), F32),
@@ -330,15 +369,27 @@
                 vmem(tiles, F32),
                 vmem(tiles, F32),
                 vmem(slab, F32),
-                vmem(slab, F32),
-                dma((12,)), dma((3,)), dma((3,)), dma((3,)), dma((2,)), dma((2,)),
-                dma((NT,)), dma((NT,)), dma((NT + 3,)),
+                dma((9,)), dma((3,)), dma((3,)), dma((3,)), dma((2,)), dma((2,)),
+                dma((NT,)), dma((NT,)), dma((NT + 1,)), pltpu.SemaphoreType.REGULAR((2,)),
             ],
             compiler_params=pltpu.CompilerParams(
-                collective_id=0, has_side_effects=True, vmem_limit_bytes=40 * 2**20
+                collective_id=0, has_side_effects=True, vmem_limit_bytes=63 * 2**20
             ),
-        )(gradient, momentum, params, *[jnp.asarray(a) for a in consts])
-        return new_w, new_m
+        )(gradient, momentum, *[jnp.asarray(a) for a in consts[:4]])
+        return pl.pallas_call(
+            last,
+            out_shape=(
+                jax.ShapeDtypeStruct(params.shape, F32),
+                jax.ShapeDtypeStruct(momentum.shape, F32),
+            ),
+            in_specs=[pl.BlockSpec(memory_space=pl.ANY)] * 5,
+            out_specs=(pl.BlockSpec(memory_space=pl.ANY),) * 2,
+            scratch_shapes=[
+                vmem((NT, *chunk), F32), vmem(slab, F32), vmem(slab, F32),
+                *[vmem(a.shape, BF16) for a in consts[4:]], vmem(slab, F32), dma((7,)), dma((6,)),
+            ],
+            compiler_params=pltpu.CompilerParams(vmem_limit_bytes=63 * 2**20),
+        )(totals, new_m, params, *[jnp.asarray(a) for a in consts[4:]])
 
     return jax.shard_map(
         per_device,

time: 52.5 us -> 41.5 us (0.79)
  local copies, waits for them, and re-layouts: 10.4 us -> 0 us
    unnamed x20 -> x0, local copies, waits for them, and re-layouts: 10.4 us -> none
    pallas_call x1 -> x2, Pallas kernels: 40.9 us -> 40.7 us  [the longest x1 37.8 us: per_device(): pl.pallas_call(kernel, out_shape=(jax.ShapeDtypeStruct((NT, *chunk), F32)...]
where the time goes in v2:
time: 41.5 us; the launch traced here: 41.4 us
  Pallas kernels  40.7 us (98%)
  between operations  0.64 us (2%)
    pallas_call x1, Pallas kernels, per_device(): pl.pallas_call(kernel, out_shape=(jax.ShapeDtypeStruct((NT, *chunk), F32)...  37.8 us
    pallas_call x1, Pallas kernels, per_device(): pl.pallas_call(last, out_shape=(jax.ShapeDtypeStruct(params.shape, F32),...  2.95 us

profile of v2, /device:TPU:8, one launch (start us, length us, event | category | flops | bytes accessed | tf_op | source)
XLA Modules:
  0.0 41.4 jit_solution(16415804689441917099)
XLA Ops:
  0.6 37.8 %shard_map.104 = (f32[10,8,128]{2,1,0:T(8,128)}, f32[1,128,1280]{2,1,0:T(8,128)}) custom-call(bf16[1,1,128,5120]{3,2,1,0:T(8,128)(2,1)} %g_hbm.1, f32[1,128,1280]{2,1,0:T(8,128)} %m_hbm.1, bf16[512,256]{1,0:T(8,128)(2,1)} %constant.12.clone.c_right, bf16[64,256]{1,0:T(8,128)(2,1)} %constant.13.clone.c_left, bf16[128,384]{1,0:T(8,128)(2,1)} %constant.14.clone.c_pl, ...), custom_call_target="tpu_custom_call" | custom-call | tf_op jit(solution)/shard_map/pallas_call | solution.py:348
  38.4 2.9 %shard_map.105 = (f32[128,1280]{1,0:T(8,128)}, f32[1,128,1280]{2,1,0:T(8,128)}) custom-call(f32[10,8,128]{2,1,0:T(8,128)} %get-tuple-element.4.refs_0_, f32[1,128,1280]{2,1,0:T(8,128)} %get-tuple-element.5.refs_1_, f32[128,1280]{1,0:T(8,128)} %refs_2_.1, bf16[128,96]{1,0:T(8,128)(2,1)} %constant.16.clone.refs_3_, bf16[384,512]{1,0:T(8,128)(2,1)} %constant.17.clone.refs_4_), custom_call_target="tpu_custom_call" | custom-call | tf_op jit(solution)/shard_map/pallas_call | solution.py:379

commit v3 on v2

--- a/solution.py
+++ b/solution.py
@@ -10,8 +10,9 @@
 F32, BF16 = jnp.float32, jnp.bfloat16
 TILE, KEEP = 128, 32
 NXH, NZ, NY = 2, 12, 8
-FIRST, LINES = 7, 5
-ROWS_XY = [(i, (FIRST + j) % NY) for i in range(NXH) for j in range(LINES)]
+FIRST, NC = 7, 5
+ROWS_XY = [(0, (FIRST + j) % NY) for j in range(NC)]
+FORWARD = {0: (11, 10, 9, 8), 1: (7,), 2: (3, 4, 5, 6)}
 NT = 10
 
 
@@ -77,9 +78,9 @@
     tail = z[:, 256:384]
     tail = tail[:16] + pltpu.roll(tail[16:], 64, 1)
     return (
-        z[:, :128].reshape(4, 8, 128),
-        z[:, 128:256].reshape(4, 8, 128),
-        tail.reshape(2, 8, 128),
+        z[:, :128].reshape(2, 16, 128),
+        z[:, 128:256].reshape(2, 16, 128),
+        tail.reshape(1, 16, 128),
     )
 
 
@@ -89,7 +90,7 @@
     gs, ms, right, left, p_left, p_right,
     cf, rc, sa, ra, sb, rb, sc, rt,
     gst, rg, xs, xt, om,
-    load_sem, core_s, core_r, a_sem, b_sem, c_sem, x_s, x_r, out_sem, in_sem,
+    load_sem, core_s, core_r, a_sem, b_sem, c_sem, x_s, x_r, out_sem, in_sem, f_sem,
 ):
     rep, f = lax.axis_index("rep"), lax.axis_index("fsdp")
     xh, z, y = rep // (NZ * NY), (rep // NY) % NZ, rep % NY
@@ -101,8 +102,9 @@
     sibling = device(xh, z, y, xl, 1 - c)
     across = device(xh, z, y, 1 - xl, c)
     line = (y - FIRST + NY) % NY
-    owner = line < LINES
-    mine = jnp.where(owner, xh * LINES + line, 0)
+    owner = jnp.logical_and(xh == 0, line < NC)
+    mine = jnp.where(owner, line, 0)
+    early = z < len(FORWARD)
     chip = (xh * NY + y) * 2 + xl
 
     blocks = [f, (1 - xl) * 2 + c, xl * 2 + 1 - c, (1 - xl) * 2 + 1 - c]
@@ -118,7 +120,7 @@
             [(c_right, right), (c_left, left), (m_hbm.at[0], ms), (c_pl, p_left), (c_pr, p_right)]
         )
     ]
-    for copy in consts[:1] + loads + consts[1:]:
+    for copy in consts[:1] + loads[2:] + consts[1:2] + loads[:2] + consts[2:]:
         copy.start()
 
     barrier = pltpu.get_barrier_semaphore()
@@ -153,17 +155,17 @@
     zs = rows_of(jnp.concatenate(ys, 1), left[...])
     for i in (2, 3):
         q = chunks_of(zs[:, 384 * (i - 2) : 384 * (i - 1)])
-        cf[i, 0:4], cf[i, 4:8], cf[i, 8:10] = q
+        cf[i, 0:2], cf[i, 2:4], cf[i, 4:5] = q
 
     @pl.when(c == 0)
     def _():
         @pl.when(owner)
         def _():
-            pl.semaphore_wait(barrier, 4 * NT - 1)
+            pl.semaphore_wait(barrier, 4 * NC - 1)
 
         @pl.when(jnp.logical_not(owner))
         def _():
-            pl.semaphore_wait(barrier, 4 * NT + 3)
+            pl.semaphore_wait(barrier, 4 * NC + 3)
 
         signal(sibling, in_sem.at[0])
 
@@ -193,9 +195,9 @@
     core0.wait_recv()
     for i in (0, 1):
         q = chunks_of(zs[:, 384 * i : 384 * (i + 1)])
-        sa[i, 0:4] = q[0] + rc[i, 0:4]
-        sa[i, 4:8] = q[1] + rc[i, 4:8]
-        sa[i, 8:10] = q[2] + rc[i, 8:10]
+        sa[i, 0:2] = q[0] + rc[i, 0:2]
+        sa[i, 2:4] = q[1] + rc[i, 2:4]
+        sa[i, 4:5] = q[2] + rc[i, 4:5]
 
     for i in range(2):
         for j, (ox, oy) in enumerate(ROWS_XY):
@@ -243,19 +245,38 @@
         def _():
             pl.semaphore_wait(in_sem.at[1], 1)
 
-        for dz in list(range(1, 7)) + list(range(11, 6, -1)):
-            send(sb, rb.at[z], b_sem.at[0], b_sem.at[1], device(xh, (z + dz) % NZ, y, xl, c)).start()
-        send(rb.at[pl.ds(0, 11)], rb.at[pl.ds(0, 11)], b_sem.at[0], b_sem.at[1], sibling).wait_recv()
-        total = rb[0]
-        for i in range(1, NZ):
-            total = total + rb[i]
-        sc[...] = total
-        rt[mine] = total
-        for dx in range(2):
-            for dy in range(NY):
-                if dx or dy:
-                    to = device((xh + dx) % 2, z, (y + dy) % NY, xl, c)
-                    send(sc, rt.at[mine], c_sem.at[0], c_sem.at[1], to).start()
+        for k in FORWARD:
+
+            @pl.when(z != k)
+            def _():
+                send(sb, rb.at[z], b_sem.at[0], b_sem.at[1], device(xh, k, y, xl, c)).start()
+
+        @pl.when(early)
+        def _():
+            send(rb.at[pl.ds(0, 11)], rb.at[pl.ds(0, 11)], b_sem.at[0], b_sem.at[1], sibling).wait_recv()
+            total = rb[0]
+            for i in range(1, NZ):
+                total = total + rb[i]
+            sc[...] = total
+
+        @pl.when(jnp.logical_not(early))
+        def _():
+            send(sc, sc, f_sem.at[0], f_sem.at[1], sibling).wait_recv()
+
+        rt[mine] = sc[...]
+        for oy in (0, 1, 7, 2, 6, 3, 5, 4):
+            for ox in range(NXH):
+
+                @pl.when(jnp.logical_or(xh != ox, y != oy))
+                def _():
+                    send(sc, rt.at[mine], c_sem.at[0], c_sem.at[1], device(ox, z, oy, xl, c)).start()
+
+        for k, others in FORWARD.items():
+
+            @pl.when(z == k)
+            def _():
+                for other in others:
+                    send(sc, sc, f_sem.at[0], f_sem.at[1], device(xh, other, y, xl, c)).start()
 
     core2.wait_recv()
     consts[3].wait()
@@ -273,7 +294,7 @@
 
     @pl.when(owner)
     def _():
-        send(rt.at[pl.ds(0, 9)], rt.at[pl.ds(0, 9)], c_sem.at[0], c_sem.at[1], sibling).wait_recv()
+        send(rt.at[pl.ds(0, NC - 1)], rt.at[pl.ds(0, NC - 1)], c_sem.at[0], c_sem.at[1], sibling).wait_recv()
 
     @pl.when(jnp.logical_not(owner))
     def _():
@@ -288,8 +309,21 @@
 
     @pl.when(owner)
     def _():
-        send(sa.at[0, pl.ds(0, 9)], sa.at[0, pl.ds(0, 9)], a_sem.at[0], a_sem.at[2], sibling).wait_send()
-        send(rb.at[pl.ds(0, 11)], rb.at[pl.ds(0, 11)], b_sem.at[0], b_sem.at[1], sibling).wait_send()
+        send(sa.at[0, pl.ds(0, NC - 1)], sa.at[0, pl.ds(0, NC - 1)], a_sem.at[0], a_sem.at[2], sibling).wait_send()
+        few = pl.ds(0, len(FORWARD) - 1)
+        send(rb.at[few], rb.at[few], b_sem.at[0], b_sem.at[1], sibling).wait_send()
+
+        @pl.when(jnp.logical_not(early))
+        def _():
+            send(sb, sb, b_sem.at[0], b_sem.at[1], sibling).wait_send()
+
+        for k, others in FORWARD.items():
+
+            @pl.when(z == k)
+            def _():
+                all_of = pl.ds(0, len(others))
+                send(rb.at[all_of], rb.at[all_of], f_sem.at[0], f_sem.at[1], sibling).wait_send()
+
         send(ra.at[pl.ds(0, 15)], ra.at[pl.ds(0, 15)], c_sem.at[0], c_sem.at[1], sibling).wait_send()
 
     @pl.when(jnp.logical_not(owner))
@@ -312,9 +346,9 @@
         copy.start()
     for copy in loads[:4]:
         copy.wait()
-    tail = rt[8:10].reshape(16, 128)
+    tail = rt[4]
     zt = jnp.concatenate(
-        [rt[0:4].reshape(32, 128), rt[4:8].reshape(32, 128), jnp.concatenate([tail, pltpu.roll(tail, 64, 1)], 0)], 1
+        [rt[0:2].reshape(32, 128), rt[2:4].reshape(32, 128), jnp.concatenate([tail, pltpu.roll(tail, 64, 1)], 0)], 1
     )
     z1, z2 = split(zt)
     v1, v2 = split(dot(d_left[...], jnp.concatenate([z1, z2, z1], 0)))
@@ -339,7 +373,7 @@
     def per_device(gradient, momentum, params):
         vmem, dma = pltpu.VMEM, pltpu.SemaphoreType.DMA
         tiles = (NT, TILE, TILE)
-        chunk = (8, 128)
+        chunk = (16, 128)
         slab = (TILE, NT * TILE)
 
         def last(*refs):
@@ -348,7 +382,7 @@
         totals, new_m = pl.pallas_call(
             kernel,
             out_shape=(
-                jax.ShapeDtypeStruct((NT, *chunk), F32),
+                jax.ShapeDtypeStruct((NC, *chunk), F32),
                 jax.ShapeDtypeStruct(momentum.shape, F32),
             ),
             in_specs=[pl.BlockSpec(memory_space=pl.ANY)] * 6,
@@ -356,21 +390,21 @@
             scratch_shapes=[
                 vmem((4, *slab), BF16), vmem(slab, F32),
                 *[vmem(a.shape, BF16) for a in consts[:4]],
-                vmem((4, NT, *chunk), F32),
-                vmem((2, NT, *chunk), F32),
-                vmem((2, NT, *chunk), F32),
+                vmem((4, NC, *chunk), F32),
+                vmem((2, NC, *chunk), F32),
+                vmem((2, NC, *chunk), F32),
                 vmem((32, *chunk), F32),
                 vmem(chunk, F32),
                 vmem((NZ, *chunk), F32),
                 vmem(chunk, F32),
-                vmem((NT, *chunk), F32),
+                vmem((NC, *chunk), F32),
                 vmem((2, *tiles), F32),
                 vmem((2, *tiles), F32),
                 vmem(tiles, F32),
                 vmem(tiles, F32),
                 vmem(slab, F32),
                 dma((9,)), dma((3,)), dma((3,)), dma((3,)), dma((2,)), dma((2,)),
-                dma((NT,)), dma((NT,)), dma((NT + 1,)), pltpu.SemaphoreType.REGULAR((2,)),
+                dma((NT,)), dma((NT,)), dma((NT + 1,)), pltpu.SemaphoreType.REGULAR((2,)), dma((2,)),
             ],
             compiler_params=pltpu.CompilerParams(
                 collective_id=0, has_side_effects=True, vmem_limit_bytes=63 * 2**20
@@ -385,7 +419,7 @@
             in_specs=[pl.BlockSpec(memory_space=pl.ANY)] * 5,
             out_specs=(pl.BlockSpec(memory_space=pl.ANY),) * 2,
             scratch_shapes=[
-                vmem((NT, *chunk), F32), vmem(slab, F32), vmem(slab, F32),
+                vmem((NC, *chunk), F32), vmem(slab, F32), vmem(slab, F32),
                 *[vmem(a.shape, BF16) for a in consts[4:]], vmem(slab, F32), dma((7,)), dma((6,)),
             ],
             compiler_params=pltpu.CompilerParams(vmem_limit_bytes=63 * 2**20),

time: 41.5 us -> 40.3 us (0.971)
  the two profiles are of different devices: /device:TPU:8 before, /device:TPU:20 now
where the time goes in v3:
time: 40.3 us; the launch traced here: 40.1 us
  Pallas kernels  39.5 us (98%)
  between operations  0.64 us (2%)
    pallas_call x1, Pallas kernels, per_device(): pl.pallas_call(kernel, out_shape=(jax.ShapeDtypeStruct((NC, *chunk), F32)...  36.5 us
    pallas_call x1, Pallas kernels, per_device(): pl.pallas_call(last, out_shape=(jax.ShapeDtypeStruct(params.shape, F32),...  2.94 us

profile of v3, /device:TPU:20, one launch (start us, length us, event | category | flops | bytes accessed | tf_op | source)
XLA Modules:
  0.0 40.1 jit_solution(10930286843549775749)
XLA Ops:
  0.6 36.5 %shard_map.104 = (f32[5,16,128]{2,1,0:T(8,128)}, f32[1,128,1280]{2,1,0:T(8,128)}) custom-call(bf16[1,1,128,5120]{3,2,1,0:T(8,128)(2,1)} %g_hbm.1, f32[1,128,1280]{2,1,0:T(8,128)} %m_hbm.1, bf16[512,256]{1,0:T(8,128)(2,1)} %constant.12.clone.c_right, bf16[64,256]{1,0:T(8,128)(2,1)} %constant.13.clone.c_left, bf16[128,384]{1,0:T(8,128)(2,1)} %constant.14.clone.c_pl, ...), custom_call_target="tpu_custom_call" | custom-call | tf_op jit(solution)/shard_map/pallas_call | solution.py:382
  37.1 2.9 %shard_map.105 = (f32[128,1280]{1,0:T(8,128)}, f32[1,128,1280]{2,1,0:T(8,128)}) custom-call(f32[5,16,128]{2,1,0:T(8,128)} %get-tuple-element.4.refs_0_, f32[1,128,1280]{2,1,0:T(8,128)} %get-tuple-element.5.refs_1_, f32[128,1280]{1,0:T(8,128)} %refs_2_.1, bf16[128,96]{1,0:T(8,128)(2,1)} %constant.16.clone.refs_3_, bf16[384,512]{1,0:T(8,128)(2,1)} %constant.17.clone.refs_4_), custom_call_target="tpu_custom_call" | custom-call | tf_op jit(solution)/shard_map/pallas_call | solution.py:413
